TPU v7x, 32 devices: a whole 2x2x4 slice. The times are simulated.
32 devices in a mesh: groups: 2 (over x), pair: 16 (over z, y, core).
Axes of the slice: x: 2, y: 2, z: 4, core: 2. Of those that a mesh axis runs over, the one named last changes fastest.
Arguments:
- chol: bfloat16 [2048, 262144], P('groups', 'pair'), parts along dimension 0, may hold values from -0.3125 to 0.3125
- walkers: bfloat16 [64, 512, 128], P(('groups', 'pair')), parts along dimension 0, may hold values from -6 to 6
- trial: bfloat16 [1024, 128], P('groups'), parts along dimension 0, may hold values from -0.5 to 0.5
- one_body: bfloat16 [1024, 512], P('groups'), parts along dimension 0, may hold values from -0.625 to 0.625
- fields: float32 [64, 1024], P(('groups', 'pair')), parts along dimension 0, may hold values from -6 to 6
- src_shift: int32 [64], P(('groups', 'pair')), parts along dimension 0, may hold values from -1 to 1
- src_slot: int32 [64], P(('groups', 'pair')), parts along dimension 0, may hold values from 0 to 1
Outputs:
- next_walkers: bfloat16 [64, 512, 128], P(('groups', 'pair')), parts along dimension 0
There are 2 independent parts, one for each index of `groups`. A program takes and returns all parts, laid end to end along the dimension named above; each array names one. Nothing has to cross between parts.
All inputs are finite; a program needn't handle non-finite values.
Results may differ from a plain program's by a relative error of at most 0.012.
Values may be sent and summed in bfloat16 or wider, within the bound.
A program may use at most 64 MiB of HBM per device.

v0:
```python
import jax
import jax.numpy as jnp
from jax import lax
from jax.sharding import PartitionSpec as P

TERMS = 6


sqrt_tau = 0.1
bias_cap = 1.0


def padded_2(block, sides, width):
    for axis, dim in sides:
        count = lax.axis_size(axis)
        forward = [(i, i + 1) for i in range(count - 1)]
        forward.append((count - 1, 0))
        backward = [(target, source) for source, target in forward]
        low = lax.ppermute(
            lax.slice_in_dim(block, block.shape[dim] - width, None, axis=dim), axis, forward
        )
        high = lax.ppermute(lax.slice_in_dim(block, 0, width, axis=dim), axis, backward)
        block = jnp.concatenate([low, block, high], axis=dim)
    return block


def shards(chol, walkers, trial, one_body, fields, src_shift, src_slot):
    w_local = walkers.shape[0]
    orbitals = walkers.shape[1]
    moved = lax.all_to_all(walkers, "pair", split_axis=1, concat_axis=0, tiled=True)
    formed = jnp.einsum("wia,ka->wik", moved, trial, preferred_element_type=jnp.float32)
    green_rows = formed.astype(jnp.bfloat16).reshape(moved.shape[0], moved.shape[1] * orbitals)
    partial_bias = lax.dot_general(
        green_rows, chol, (((1,), (1,)), ((), ())), preferred_element_type=jnp.float32
    )
    summed = lax.psum(partial_bias, "pair")
    every_field = lax.all_gather(fields, "pair", axis=0, tiled=True)
    shift = (every_field - jnp.clip(sqrt_tau * summed, -bias_cap, bias_cap)).astype(jnp.bfloat16)
    local_potential = (sqrt_tau * jnp.dot(shift, chol, preferred_element_type=jnp.float32)).astype(
        jnp.bfloat16
    )
    own_potential = lax.all_to_all(local_potential, "pair", split_axis=0, concat_axis=1, tiled=True)
    amat = own_potential.astype(jnp.float32).reshape(w_local, orbitals, orbitals) + one_body.astype(
        jnp.float32
    )
    amat = amat.astype(jnp.bfloat16)
    term = walkers
    total = walkers.astype(jnp.float32)
    for order in range(1, TERMS):
        product = jnp.einsum("wik,wka->wia", amat, term, preferred_element_type=jnp.float32) / order
        total = total + product
        term = product.astype(jnp.bfloat16)
    propagated = total.astype(jnp.bfloat16)
    padded = padded_2(propagated, (("pair", 0),), w_local)
    position = (src_shift + 1) * w_local + src_slot
    return jnp.take(padded, position, axis=0)


def solution(mesh):
    placed = (
        P("groups", "pair"),
        P(("groups", "pair"), None, None),
        P("groups", None),
        P("groups", None),
        P(("groups", "pair"), None),
        P(("groups", "pair")),
        P(("groups", "pair")),
    )
    return jax.shard_map(
        shards,
        mesh=mesh,
        in_specs=placed,
        out_specs=P(("groups", "pair"), None, None),
        check_vma=False,
    )
```

profile of v0, /device:TPU:0, one launch (start us, length us, event | category | flops | bytes accessed | tf_op | source)
XLA Modules:
  0.0 200.9 jit_solution(3262210192182722894)
XLA Ops:
  6.5 1.3 copy.10
  7.8 17.2 %all_to_all.31 = bf16[2,512,128]{2,0,1:T(2,128)(2,1)S(1)} all-to-all(bf16[2,512,128]{2,0,1:T(2,128)(2,1)S(1)} %copy.10), channel_id=1, replica_groups=mesh['groups'=2,'pair'=16] {'pair'}, dimensions={1} | all-to-all | bytes 524288 | tf_op jit(solution)/shard_map/all_to_all | solution.py:30
  25.5 0.6 copy.13
  26.1 15.8 %fusion.14 = f32[32,1024]{1,0:T(8,128)} fusion(bf16[32,16384]{1,0:T(8,128)(2,1)S(1)} %bitcast.22, bf16[1024,16384]{1,0:T(8,128)(2,1)} %param.7), kind=kOutput, calls=%fused_computation.29 | convolution fusion | flops 1073741824 | bytes 34734080 | tf_op jit(solution)/shard_map/dot_general | solution.py:33
  41.9 19.1 %all-gather = f32[16,2,1024]{2,1,0:T(2,128)S(1)} all-gather(f32[1,2,1024]{2,1,0:T(2,128)S(1)} %bitcast.26), channel_id=1, replica_groups=mesh['groups'=2,'pair'=16] {'pair'}, dimensions={0}, use_global_device_ids=true | all-gather | bytes 139264 | tf_op jit(solution)/shard_map/all_gather | solution.py:37
  61.1 66.2 %all-reduce.2.cloned.1.call-done = f32[32,1024]{1,0:T(8,128)} async-done(((f32[32,1024]{1,0:T(8,128)}), f32[32,1024]{1,0:T(8,128)}) %all-reduce.2.cloned.1.call-update) | async-done | bytes 131088 | tf_op jit(solution)/shard_map/psum | solution.py:36
  127.3 16.5 %fusion = bf16[32,16384]{1,0:T(8,128)(2,1)S(1)} fusion(bf16[1024,16384]{1,0:T(8,128)(2,1)} %param.7, f32[32,1024]{1,0:T(8,128)S(1)} %reshape.28, f32[32,1024]{1,0:T(8,128)} %all-reduce.2.cloned.1.call-done), kind=kOutput, calls=%fused_computation.2 | convolution fusion | flops 1074921472 | bytes 34865152 | tf_op jit(solution)/shard_map/dot_general | solution.py:39
  143.8 1.5 all_to_all.27
  145.3 6.4 %all-to-all-start.1 = ((bf16[16,2,16384]{2,1,0:T(2,128)(2,1)}), bf16[16,2,16384]{2,1,0:T(2,128)(2,1)S(1)}, u32[]{:S(2)}, u32[]{:S(2)}) async-start(bf16[16,2,16384]{2,1,0:T(2,128)(2,1)} %all_to_all.27), calls=%async_computation.1 | async-start | bytes 2097152 | tf_op jit(solution)/shard_map/all_to_all | solution.py:42
  151.8 22.8 %all-to-all-done.1 = bf16[16,2,16384]{2,1,0:T(2,128)(2,1)S(1)} async-done(((bf16[16,2,16384]{2,1,0:T(2,128)(2,1)}), bf16[16,2,16384]{2,1,0:T(2,128)(2,1)S(1)}, u32[]{:S(2)}, u32[]{:S(2)}) %all-to-all-start.1) | async-done | bytes 1048608 | tf_op jit(solution)/shard_map/all_to_all | solution.py:42
  174.6 0.9 convert_bitcast_fusion
  175.5 2.5 %copy.12 = f32[2,16,16384]{2,1,0:T(8,128)} copy(f32[2,16,16384]{2,0,1:T(2,128)S(1)} %convert_bitcast_fusion) | data formatting | bytes 4194304 | tf_op jit(solution)/shard_map/convert_element_type | solution.py:43
  178.0 1.7 reshape.17
  180.2 0.5 copy-done.1
  180.7 0.4 fusion.15
  181.2 0.4 convolution_multiply_fusion.4
  181.6 0.4 convolution_multiply_fusion.3
  182.0 0.4 convolution_multiply_fusion.2
  182.5 0.5 fusion.2
  183.0 0.7 collective-permute-start
  183.6 4.8 %collective-permute-start.1 = (bf16[2,512,128]{2,1,0:T(8,128)(2,1)S(1)}, bf16[2,512,128]{2,1,0:T(8,128)(2,1)S(1)}, u32[]{:S(2)}, u32[]{:S(2)}) collective-permute-start(bf16[2,512,128]{2,1,0:T(8,128)(2,1)S(1)} %fusion.2), channel_id=1, source_target_pairs={{1,0},{2,1},{3,2},{4,3},{5,4},{6,5},{7,6},{8,7},{9,8},{10,9},{11,1... | collective-permute-start | bytes 786440 | tf_op jit(solution)/shard_map/ppermute | solution.py:22
  188.5 4.1 %collective-permute-done = bf16[2,512,128]{2,1,0:T(8,128)(2,1)S(1)} collective-permute-done((bf16[2,512,128]{2,1,0:T(8,128)(2,1)S(1)}, bf16[2,512,128]{2,1,0:T(8,128)(2,1)S(1)}, u32[]{:S(2)}, u32[]{:S(2)}) %collective-permute-start) | collective-permute-done | bytes 262176 | tf_op jit(solution)/shard_map/ppermute | solution.py:19
  192.7 0.6 gather_fusion
  193.3 0.8 broadcast_select_fusion
  (22 shorter events, 1.3 us)
Async XLA Ops:
  6.5 18.5 %copy-start = (bf16[512,128]{1,0:T(8,128)(2,1)S(1)}, bf16[512,128]{1,0:T(8,128)(2,1)}, u32[]{:S(2)}) copy-start(bf16[512,128]{1,0:T(8,128)(2,1)} %param.9) | copy-start | bytes 393220
  6.5 120.8 %all-reduce.2.cloned.1.call-start = ((), (), s32[]{:S(2)}) async-start(), calls=%async_computation.2 | async-start | bytes 262144 | tf_op jit(solution)/shard_map/psum | solution.py:36
  26.1 15.8 %copy-start.3 = (f32[2,1024]{1,0:T(2,128)S(1)}, f32[2,1024]{1,0:T(2,128)}, u32[]{:S(2)}) copy-start(f32[2,1024]{1,0:T(2,128)} %param.11) | copy-start | bytes 24580
  143.8 7.9 %copy-start.2 = (bf16[512,512]{1,0:T(8,128)(2,1)S(1)}, bf16[512,512]{1,0:T(8,128)(2,1)}, u32[]{:S(2)}) copy-start(bf16[512,512]{1,0:T(8,128)(2,1)} %param.10) | copy-start | bytes 1572868
  145.3 29.3 %all-to-all-start.1 = ((bf16[16,2,16384]{2,1,0:T(2,128)(2,1)}), bf16[16,2,16384]{2,1,0:T(2,128)(2,1)S(1)}, u32[]{:S(2)}, u32[]{:S(2)}) async-start(bf16[16,2,16384]{2,1,0:T(2,128)(2,1)} %all_to_all.27), calls=%async_computation.1 | async-start | bytes 2097152 | tf_op jit(solution)/shard_map/all_to_all | solution.py:42
  179.8 1.0 copy-start.1
  182.5 6.0 %copy-start.4 = (s32[2]{0:T(128)S(1)}, s32[2]{0:T(128)}, u32[]{:S(2)}) copy-start(s32[2]{0:T(128)} %param.13) | copy-start | bytes 28
  182.5 6.0 %copy-start.5 = (s32[2]{0:T(128)S(1)}, s32[2]{0:T(128)}, u32[]{:S(2)}) copy-start(s32[2]{0:T(128)} %param.12) | copy-start | bytes 28
  183.0 9.6 %collective-permute-start = (bf16[2,512,128]{2,1,0:T(8,128)(2,1)S(1)}, bf16[2,512,128]{2,1,0:T(8,128)(2,1)S(1)}, u32[]{:S(2)}, u32[]{:S(2)}) collective-permute-start(bf16[2,512,128]{2,1,0:T(8,128)(2,1)S(1)} %fusion.2), channel_id=1, source_target_pairs={{0,1},{1,2},{2,3},{3,4},{4,5},{5,6},{6,7},{7,8},{8,9},{9,10},{10,1... | collective-permute-start | bytes 786440 | tf_op jit(solution)/shard_map/ppermute | solution.py:19
  183.6 9.0 %collective-permute-start.1 = (bf16[2,512,128]{2,1,0:T(8,128)(2,1)S(1)}, bf16[2,512,128]{2,1,0:T(8,128)(2,1)S(1)}, u32[]{:S(2)}, u32[]{:S(2)}) collective-permute-start(bf16[2,512,128]{2,1,0:T(8,128)(2,1)S(1)} %fusion.2), channel_id=1, source_target_pairs={{1,0},{2,1},{3,2},{4,3},{5,4},{6,5},{7,6},{8,7},{9,8},{10,9},{11,1... | collective-permute-start | bytes 786440 | tf_op jit(solution)/shard_map/ppermute | solution.py:22
Sparse Core Ops, SparseCore 0:
  42.0 85.2 all-reduce.1
where the time goes:
time: 202 us; the launch traced here: 201 us
  waiting for transfers between devices  93.1 us (46%)
  blocking collectives  36.3 us (18%)
  matrix products  34.9 us (17%)
  between operations  13.6 us (7%)
  starting transfers between devices  11.9 us (6%)
  local copies, waits for them, and re-layouts  8.9 us (4%)
  other arithmetic  2.3 us (1%)
    psum x1, waiting for transfers between devices, shards(): summed = lax.psum(partial_bias, 'pair')  66.2 us
    all_to_all x1, waiting for transfers between devices, shards(): lax.all_to_all(local_potential, 'pair', split_axis=0, concat_axis=1, tile...  22.8 us
    all_gather x1, blocking collectives, shards(): every_field = lax.all_gather(fields, 'pair', axis=0, tiled=True)  19.1 us
    all_to_all x1, blocking collectives, shards(): lax.all_to_all(walkers, 'pair', split_axis=1, concat_axis=0, tiled=True)  17.2 us
    dot_general x1, matrix products, shards(): jnp.dot(shift, chol, preferred_element_type=jnp.float32)  16.5 us
    dot_general x1, matrix products, shards(): lax.dot_general(green_rows, chol, (((1,), (1,)), ((), ())), preferred_ele...  15.8 us
    all_to_all x1, starting transfers between devices, shards(): lax.all_to_all(local_potential, 'pair', split_axis=0, concat_axis=1, tile...  6.36 us
    ppermute x1, starting transfers between devices, padded_2(): lax.ppermute(lax.slice_in_dim(block, 0, width, axis=dim), axis, backward)  4.85 us
  transfers between devices with their start and end apart: 4, of which 3 were waited for; matrix products, arithmetic and copies ran while one was open for 0% of the time, Pallas kernels for 0%

commit v1 on v0

--- a/solution.py
+++ b/solution.py
@@ -24,36 +24,46 @@
     return block
 
 
+def taylor(amat, block):
+    term = block
+    total = block.astype(jnp.float32)
+    for order in range(1, TERMS):
+        product = jnp.einsum("wik,wka->wia", amat, term, preferred_element_type=jnp.float32) / order
+        total = total + product
+        term = product.astype(jnp.bfloat16)
+    return total.astype(jnp.bfloat16)
+
+
 def shards(chol, walkers, trial, one_body, fields, src_shift, src_slot):
-    w_local = walkers.shape[0]
-    orbitals = walkers.shape[1]
+    w_local, orbitals, _ = walkers.shape
+    count = lax.axis_size("pair")
+    me = lax.axis_index("pair")
     moved = lax.all_to_all(walkers, "pair", split_axis=1, concat_axis=0, tiled=True)
+    source = (me + src_shift + count) % count * w_local + src_slot
+    sources = lax.all_gather(source, "pair", axis=0, tiled=True)
+    padded = padded_2(walkers, (("pair", 0),), w_local)
+    parents = jnp.take(padded, (src_shift + 1) * w_local + src_slot, axis=0)
     formed = jnp.einsum("wia,ka->wik", moved, trial, preferred_element_type=jnp.float32)
     green_rows = formed.astype(jnp.bfloat16).reshape(moved.shape[0], moved.shape[1] * orbitals)
     partial_bias = lax.dot_general(
         green_rows, chol, (((1,), (1,)), ((), ())), preferred_element_type=jnp.float32
     )
-    summed = lax.psum(partial_bias, "pair")
-    every_field = lax.all_gather(fields, "pair", axis=0, tiled=True)
-    shift = (every_field - jnp.clip(sqrt_tau * summed, -bias_cap, bias_cap)).astype(jnp.bfloat16)
-    local_potential = (sqrt_tau * jnp.dot(shift, chol, preferred_element_type=jnp.float32)).astype(
+    pieces = lax.all_to_all(
+        partial_bias.reshape(count, w_local, -1), "pair", split_axis=0, concat_axis=0, tiled=True
+    )
+    summed = jnp.sum(pieces, axis=0)
+    shift = (fields - jnp.clip(sqrt_tau * summed, -bias_cap, bias_cap)).astype(jnp.bfloat16)
+    spread = jnp.broadcast_to(shift[None], (count,) + shift.shape)
+    every_shift = lax.all_to_all(spread, "pair", split_axis=0, concat_axis=0, tiled=True)
+    chosen = jnp.take(every_shift.reshape(count * w_local, -1), sources, axis=0)
+    local_potential = (sqrt_tau * jnp.dot(chosen, chol, preferred_element_type=jnp.float32)).astype(
         jnp.bfloat16
     )
     own_potential = lax.all_to_all(local_potential, "pair", split_axis=0, concat_axis=1, tiled=True)
     amat = own_potential.astype(jnp.float32).reshape(w_local, orbitals, orbitals) + one_body.astype(
         jnp.float32
     )
-    amat = amat.astype(jnp.bfloat16)
-    term = walkers
-    total = walkers.astype(jnp.float32)
-    for order in range(1, TERMS):
-        product = jnp.einsum("wik,wka->wia", amat, term, preferred_element_type=jnp.float32) / order
-        total = total + product
-        term = product.astype(jnp.bfloat16)
-    propagated = total.astype(jnp.bfloat16)
-    padded = padded_2(propagated, (("pair", 0),), w_local)
-    position = (src_shift + 1) * w_local + src_slot
-    return jnp.take(padded, position, axis=0)
+    return taylor(amat.astype(jnp.bfloat16), parents)
 
 
 def solution(mesh):

time: 202 us -> 120 us (0.59)
  waiting for transfers between devices: 93.1 us -> 35.8 us
  blocking collectives: 36.3 us -> 12.3 us
  between operations: 13.6 us -> 0.92 us
  starting transfers between devices: 11.9 us -> 22.7 us
  local copies, waits for them, and re-layouts: 8.9 us -> 12.6 us
  matrix products: 34.9 us -> 32.3 us
    psum x1 -> x0, waiting for transfers between devices: 66.2 us -> none  [shards(): summed = lax.psum(partial_bias, 'pair')]
    all_to_all x1, waiting for transfers between devices: 22.8 us -> 0.01 us  [shards(): lax.all_to_all(local_potential, 'pair', split_axis=0, concat_axis=1, tile...]
    all_gather x1 -> x0, blocking collectives: 19.1 us -> none  [shards(): every_field = lax.all_gather(fields, 'pair', axis=0, tiled=True)]
    all_to_all x1 -> x0, blocking collectives: 17.2 us -> none  [shards(): lax.all_to_all(walkers, 'pair', split_axis=1, concat_axis=0, tiled=True)]
    ppermute x1, waiting for transfers between devices: 4.07 us -> 20.9 us  [padded_2(): lax.ppermute(lax.slice_in_dim(block, block.shape[dim] - width, None, axis...]
    all_to_all x0 -> x3, waiting for transfers between devices: none -> 14.9 us  [the longest x1 8.11 us: shards(): lax.all_to_all(walkers, 'pair', split_axis=1, concat_axis=0, tiled=True)]
    all_to_all x0 -> x3, starting transfers between devices: none -> 14.4 us  [the longest x1 7.39 us: shards(): lax.all_to_all(walkers, 'pair', split_axis=1, concat_axis=0, tiled=True)]
    unnamed x0 -> x1, blocking collectives: none -> 12.3 us
  transfers between devices with their start and end apart: 4 -> 6, of which waited for: 3 -> 3; matrix products, arithmetic and copies ran while one was open for 0% -> 2% of each run, Pallas kernels for 0% -> 0%
where the time goes in v1:
time: 120 us; the launch traced here: 118 us
  waiting for transfers between devices  35.8 us (30%)
  matrix products  32.3 us (27%)
  starting transfers between devices  22.7 us (19%)
  local copies, waits for them, and re-layouts  12.6 us (10%)
  blocking collectives  12.3 us (10%)
  other arithmetic  1.71 us (1%)
    ppermute x1, waiting for transfers between devices, padded_2(): lax.ppermute(lax.slice_in_dim(block, block.shape[dim] - width, None, axis...  20.9 us
    dot_general x1, matrix products, shards(): lax.dot_general(green_rows, chol, (((1,), (1,)), ((), ())), preferred_ele...  15.1 us
    dot_general x1, matrix products, shards(): jnp.dot(chosen, chol, preferred_element_type=jnp.float32)  13.8 us
    unnamed x1, blocking collectives  12.3 us
    all_to_all x1, waiting for transfers between devices, shards(): lax.all_to_all(walkers, 'pair', split_axis=1, concat_axis=0, tiled=True)  8.11 us
    all_to_all x1, starting transfers between devices, shards(): lax.all_to_all(walkers, 'pair', split_axis=1, concat_axis=0, tiled=True)  7.39 us
    all_to_all x1, waiting for transfers between devices, shards(): lax.all_to_all(spread, 'pair', split_axis=0, concat_axis=0, tiled=True)  6.83 us
    ppermute x1, starting transfers between devices, padded_2(): lax.ppermute(lax.slice_in_dim(block, 0, width, axis=dim), axis, backward)  4.3 us
  transfers between devices with their start and end apart: 6, of which 3 were waited for; matrix products, arithmetic and copies ran while one was open for 2% of the time, Pallas kernels for 0%

profile of v1, /device:TPU:0, one launch (start us, length us, event | category | flops | bytes accessed | tf_op | source)
XLA Modules:
  0.0 118.4 jit_solution(9691290148692162480)
XLA Ops:
  0.0 2.0 %copy.11 = bf16[2,512,128]{2,0,1:T(2,128)(2,1)} copy(bf16[2,512,128]{2,1,0:T(8,128)(2,1)} %param.8) | data formatting | bytes 524288 | tf_op args[1]
  2.0 7.4 %all-to-all-start = ((bf16[2,512,128]{2,0,1:T(2,128)(2,1)}), bf16[2,512,128]{2,0,1:T(2,128)(2,1)S(1)}, u32[]{:S(2)}, u32[]{:S(2)}) async-start(bf16[2,512,128]{2,0,1:T(2,128)(2,1)} %copy.11), calls=%async_computation | async-start | bytes 524288 | tf_op jit(solution)/shard_map/all_to_all | solution.py:41
  9.4 1.3 %dynamic-slice = u32[1]{0:T(128)} dynamic-slice(u32[32]{0:T(128)} %constant.81, u32[]{:T(128)S(6)} %add.76), dynamic_slice_sizes={1} | dynamic-slice | bytes 12
  11.3 8.1 %all-to-all-done = bf16[2,512,128]{2,0,1:T(2,128)(2,1)S(1)} async-done(((bf16[2,512,128]{2,0,1:T(2,128)(2,1)}), bf16[2,512,128]{2,0,1:T(2,128)(2,1)S(1)}, u32[]{:S(2)}, u32[]{:S(2)}) %all-to-all-start) | async-done | bytes 262176 | tf_op jit(solution)/shard_map/all_to_all | solution.py:41
  19.9 0.8 dot_general.27
  20.7 15.1 %fusion = f32[16,2,1024]{2,0,1:T(8,128)S(1)} fusion(bf16[1024,16384]{1,0:T(8,128)(2,1)} %param.7, bf16[16,2,16384]{2,1,0:T(2,128)(2,1)S(1)} %dot_general.27), kind=kOutput, calls=%fused_computation.2 | convolution fusion | flops 1073741824 | bytes 34734080 | tf_op jit(solution)/shard_map/dot_general | solution.py:48
  35.9 0.8 copy.14
  36.6 3.5 %all-to-all-start.1 = ((f32[16,2,1024]{2,1,0:T(2,128)}), f32[16,2,1024]{2,1,0:T(2,128)S(1)}, u32[]{:S(2)}, u32[]{:S(2)}) async-start(f32[16,2,1024]{2,1,0:T(2,128)} %copy.14), calls=%async_computation.1 | async-start | bytes 262144 | tf_op jit(solution)/shard_map/all_to_all | solution.py:51
  40.3 12.3 %all-reduce = s32[32]{0:T(128)S(1)} all-reduce(s32[32]{0:T(128)S(1)} %fusion.17), channel_id=1, replica_groups=mesh['groups'=2,'pair'=16] {'pair'}, use_global_device_ids=true, to_apply=%add | all-reduce | flops 32 | bytes 256
  52.7 0.7 broadcast_in_dim.35
  53.4 3.5 %all-to-all-start.2 = ((bf16[16,2,1024]{2,1,0:T(2,128)(2,1)}), bf16[16,2,1024]{2,1,0:T(2,128)(2,1)S(1)}, u32[]{:S(2)}, u32[]{:S(2)}) async-start(bf16[16,2,1024]{2,1,0:T(2,128)(2,1)} %broadcast_in_dim.35), calls=%async_computation.2 | async-start | bytes 131072 | tf_op jit(solution)/shard_map/all_to_all | solution.py:57
  56.9 6.8 %all-to-all-done.2 = bf16[16,2,1024]{2,1,0:T(2,128)(2,1)S(1)} async-done(((bf16[16,2,1024]{2,1,0:T(2,128)(2,1)}), bf16[16,2,1024]{2,1,0:T(2,128)(2,1)S(1)}, u32[]{:S(2)}, u32[]{:S(2)}) %all-to-all-start.2) | async-done | bytes 65568 | tf_op jit(solution)/shard_map/all_to_all | solution.py:57
  63.8 0.6 gather_fusion.1
  64.4 13.8 %fusion.2 = bf16[32,16384]{1,0:T(8,128)(2,1)S(1)} fusion(bf16[1024,16384]{1,0:T(8,128)(2,1)} %param.7, bf16[32,1024]{1,0:T(8,128)(2,1)S(1)} %gather_fusion.1, pred[32]{0:T(512)(128)(4,1)S(1)} %compare_and_fusion), kind=kOutput, calls=%fused_computation.5 | convolution fusion | flops 1074823168 | bytes 34668576 | tf_op jit(solution)/shard_map/dot_general | solution.py:59
  78.2 1.5 %all_to_all.35 = bf16[16,2,16384]{2,1,0:T(2,128)(2,1)} reshape(bf16[32,16384]{1,0:T(8,128)(2,1)S(1)} %fusion.2) | data formatting | bytes 2097152 | tf_op jit(solution)/shard_map/all_to_all | solution.py:62
  79.7 3.7 %all-to-all-start.3 = ((bf16[16,2,16384]{2,1,0:T(2,128)(2,1)}), bf16[16,2,16384]{2,1,0:T(2,128)(2,1)S(1)}, u32[]{:S(2)}, u32[]{:S(2)}) async-start(bf16[16,2,16384]{2,1,0:T(2,128)(2,1)} %all_to_all.35), calls=%async_computation.3 | async-start | bytes 2097152 | tf_op jit(solution)/shard_map/all_to_all | solution.py:62
  83.7 4.3 %collective-permute-start.1 = (bf16[2,512,128]{2,1,0:T(8,128)(2,1)S(1)}, bf16[2,512,128]{2,1,0:T(8,128)(2,1)S(1)}, u32[]{:S(2)}, u32[]{:S(2)}) collective-permute-start(bf16[2,512,128]{2,1,0:T(8,128)(2,1)S(1)} %copy-done.1), channel_id=1, source_target_pairs={{1,0},{2,1},{3,2},{4,3},{5,4},{6,5},{7,6},{8,7},{9,8},{10,9},{11,1... | collective-permute-start | bytes 786440 | tf_op jit(solution)/shard_map/ppermute | solution.py:22
  88.2 20.9 %collective-permute-done = bf16[2,512,128]{2,1,0:T(8,128)(2,1)S(1)} collective-permute-done((bf16[2,512,128]{2,1,0:T(8,128)(2,1)S(1)}, bf16[2,512,128]{2,1,0:T(8,128)(2,1)S(1)}, u32[]{:S(2)}, u32[]{:S(2)}) %collective-permute-start) | collective-permute-done | bytes 262176 | tf_op jit(solution)/shard_map/ppermute | solution.py:19
  109.2 0.6 gather_fusion
  109.8 0.9 convert_bitcast_fusion
  110.7 2.5 %copy.15 = f32[2,16,16384]{2,1,0:T(8,128)} copy(f32[2,16,16384]{2,0,1:T(2,128)S(1)} %convert_bitcast_fusion) | data formatting | bytes 4194304 | tf_op jit(solution)/shard_map/convert_element_type | solution.py:63
  113.2 1.7 %reshape.27 = f32[2,512,512]{2,1,0:T(8,128)S(1)} reshape(f32[2,16,16384]{2,1,0:T(8,128)} %copy.15) | data formatting | bytes 4194304 | tf_op jit(solution)/shard_map/convert_element_type | solution.py:63
  115.4 0.5 fusion.11
  117.2 1.1 fusion.4
  (34 shorter events, 3.0 us)
Async XLA Ops:
  0.0 19.5 %copy-start = (bf16[512,128]{1,0:T(8,128)(2,1)S(1)}, bf16[512,128]{1,0:T(8,128)(2,1)}, u32[]{:S(2)}) copy-start(bf16[512,128]{1,0:T(8,128)(2,1)} %param.9) | copy-start | bytes 393220
  2.0 17.4 %all-to-all-start = ((bf16[2,512,128]{2,0,1:T(2,128)(2,1)}), bf16[2,512,128]{2,0,1:T(2,128)(2,1)S(1)}, u32[]{:S(2)}, u32[]{:S(2)}) async-start(bf16[2,512,128]{2,0,1:T(2,128)(2,1)} %copy.11), calls=%async_computation | async-start | bytes 524288 | tf_op jit(solution)/shard_map/all_to_all | solution.py:41
  20.7 19.5 %copy-start.4 = (s32[2]{0:T(128)S(1)}, s32[2]{0:T(128)}, u32[]{:S(2)}) copy-start(s32[2]{0:T(128)} %param.13) | copy-start | bytes 28
  20.7 19.5 %copy-start.5 = (s32[2]{0:T(128)S(1)}, s32[2]{0:T(128)}, u32[]{:S(2)}) copy-start(s32[2]{0:T(128)} %param.12) | copy-start | bytes 28
  20.7 32.0 %copy-start.3 = (f32[2,1024]{1,0:T(2,128)S(1)}, f32[2,1024]{1,0:T(2,128)}, u32[]{:S(2)}) copy-start(f32[2,1024]{1,0:T(2,128)} %param.11) | copy-start | bytes 24580
  36.6 16.0 %all-to-all-start.1 = ((f32[16,2,1024]{2,1,0:T(2,128)}), f32[16,2,1024]{2,1,0:T(2,128)S(1)}, u32[]{:S(2)}, u32[]{:S(2)}) async-start(f32[16,2,1024]{2,1,0:T(2,128)} %copy.14), calls=%async_computation.1 | async-start | bytes 262144 | tf_op jit(solution)/shard_map/all_to_all | solution.py:51
  53.4 10.4 %all-to-all-start.2 = ((bf16[16,2,1024]{2,1,0:T(2,128)(2,1)}), bf16[16,2,1024]{2,1,0:T(2,128)(2,1)S(1)}, u32[]{:S(2)}, u32[]{:S(2)}) async-start(bf16[16,2,1024]{2,1,0:T(2,128)(2,1)} %broadcast_in_dim.35), calls=%async_computation.2 | async-start | bytes 131072 | tf_op jit(solution)/shard_map/all_to_all | solution.py:57
  78.2 5.2 %copy-start.1 = (bf16[2,512,128]{2,1,0:T(8,128)(2,1)S(1)}, bf16[2,512,128]{2,1,0:T(8,128)(2,1)}, u32[]{:S(2)}) copy-start(bf16[2,512,128]{2,1,0:T(8,128)(2,1)} %param.8) | copy-start | bytes 786436
  78.2 9.8 %copy-start.2 = (bf16[512,512]{1,0:T(8,128)(2,1)S(1)}, bf16[512,512]{1,0:T(8,128)(2,1)}, u32[]{:S(2)}) copy-start(bf16[512,512]{1,0:T(8,128)(2,1)} %param.10) | copy-start | bytes 1572868
  79.7 30.1 %all-to-all-start.3 = ((bf16[16,2,16384]{2,1,0:T(2,128)(2,1)}), bf16[16,2,16384]{2,1,0:T(2,128)(2,1)S(1)}, u32[]{:S(2)}, u32[]{:S(2)}) async-start(bf16[16,2,16384]{2,1,0:T(2,128)(2,1)} %all_to_all.35), calls=%async_computation.3 | async-start | bytes 2097152 | tf_op jit(solution)/shard_map/all_to_all | solution.py:62
  83.4 25.7 %collective-permute-start = (bf16[2,512,128]{2,1,0:T(8,128)(2,1)S(1)}, bf16[2,512,128]{2,1,0:T(8,128)(2,1)S(1)}, u32[]{:S(2)}, u32[]{:S(2)}) collective-permute-start(bf16[2,512,128]{2,1,0:T(8,128)(2,1)S(1)} %copy-done.1), channel_id=1, source_target_pairs={{0,1},{1,2},{2,3},{3,4},{4,5},{5,6},{6,7},{7,8},{8,9},{9,10},{10,1... | collective-permute-start | bytes 786440 | tf_op jit(solution)/shard_map/ppermute | solution.py:19
  83.7 25.4 %collective-permute-start.1 = (bf16[2,512,128]{2,1,0:T(8,128)(2,1)S(1)}, bf16[2,512,128]{2,1,0:T(8,128)(2,1)S(1)}, u32[]{:S(2)}, u32[]{:S(2)}) collective-permute-start(bf16[2,512,128]{2,1,0:T(8,128)(2,1)S(1)} %copy-done.1), channel_id=1, source_target_pairs={{1,0},{2,1},{3,2},{4,3},{5,4},{6,5},{7,6},{8,7},{9,8},{10,9},{11,1... | collective-permute-start | bytes 786440 | tf_op jit(solution)/shard_map/ppermute | solution.py:22

commit v2 on v1

--- a/solution.py
+++ b/solution.py
@@ -1,6 +1,10 @@
+import functools
+
 import jax
 import jax.numpy as jnp
 from jax import lax
+from jax.experimental import pallas as pl
+from jax.experimental.pallas import tpu as pltpu
 from jax.sharding import PartitionSpec as P
 
 TERMS = 6
@@ -34,7 +38,7 @@
     return total.astype(jnp.bfloat16)
 
 
-def shards(chol, walkers, trial, one_body, fields, src_shift, src_slot):
+def plain_shards(chol, walkers, trial, one_body, fields, src_shift, src_slot):
     w_local, orbitals, _ = walkers.shape
     count = lax.axis_size("pair")
     me = lax.axis_index("pair")
@@ -66,6 +70,212 @@
     return taylor(amat.astype(jnp.bfloat16), parents)
 
 
+MESH = pl.DeviceIdType.MESH
+
+
+def step_kernel(
+    count, chunks,
+    chol, walkers, trial, one_body, fields, onehot, weights, out,
+    held, rows_in, halo, green, picks_in, bias_out, bias_in, shift_in, flat, picks,
+    chosen, pot, pot_out, own,
+    load_sem, walk_send, walk_recv, halo_send, halo_recv, pick_send, pick_recv,
+    bias_send, bias_recv, shift_send, shift_recv, pot_send, pot_recv,
+):
+    me = lax.axis_index("pair")
+    w_local, orbitals, occupied = walkers.shape
+    rows = orbitals // count
+    total = count * w_local
+    vectors, pairs = chol.shape
+    part = pairs // chunks
+    per_part = rows // chunks
+    tall = rows // pot_out.shape[0]
+
+    def peer(k):
+        return lax.rem(me + k, count)
+
+    def remote(src, dst, send, recv, target):
+        return pltpu.make_async_remote_copy(
+            src_ref=src, dst_ref=dst, send_sem=send, recv_sem=recv,
+            device_id={"pair": target}, device_id_type=MESH,
+        )
+
+    def load(c):
+        columns = pl.ds(pl.multiple_of(c * part, part), part)
+        return pltpu.make_async_copy(chol.at[:, columns], held.at[:, columns], load_sem.at[c])
+
+    def each(low, high, body):
+        lax.fori_loop(low, high, lambda k, carry: (body(k), carry)[1], 0)
+
+    each(0, chunks, lambda c: load(c).start())
+
+    barrier = pltpu.get_barrier_semaphore()
+    each(1, count, lambda k: pl.semaphore_signal(
+        barrier, inc=1, device_id={"pair": peer(k)}, device_id_type=MESH))
+    pl.semaphore_wait(barrier, count - 1)
+
+    def block(d):
+        return pl.ds(pl.multiple_of(d * rows, rows), rows)
+
+    def walk_copy(k):
+        return remote(walkers.at[:, block(peer(k)), :], rows_in.at[me], walk_send.at[k], walk_recv.at[k], peer(k))
+
+    def pick_copy(k):
+        return remote(onehot, picks_in.at[me], pick_send.at[k], pick_recv.at[k], peer(k))
+
+    def halo_copy(side):
+        target = peer(1) if side == 0 else peer(count - 1)
+        return remote(walkers, halo.at[side], halo_send.at[side], halo_recv.at[side], target)
+
+    each(1, count, lambda k: walk_copy(k).start())
+    each(1, count, lambda k: pick_copy(k).start())
+    halo_copy(0).start()
+    halo_copy(1).start()
+    rows_in[me] = walkers[:, block(me), :]
+    picks_in[me] = onehot[...]
+    each(1, count, lambda k: walk_copy(k).wait())
+
+    arrived = rows_in[...].astype(jnp.float32).reshape(total, rows, occupied)
+    by_row = jnp.swapaxes(arrived, 0, 1).astype(jnp.bfloat16).reshape(rows * total, occupied)
+    green[...] = lax.dot_general(
+        by_row, trial[...], (((1,), (1,)), ((), ())), preferred_element_type=jnp.float32
+    ).astype(jnp.bfloat16).reshape(rows, total, orbitals)
+
+    def bias_part(c, acc):
+        load(c).wait()
+        for r in range(per_part):
+            i = c * per_part + r
+            acc = acc + lax.dot_general(
+                green[i], held[:, pl.ds(pl.multiple_of(i * orbitals, orbitals), orbitals)],
+                (((1,), (1,)), ((), ())), preferred_element_type=jnp.float32,
+            )
+        return acc
+
+    acc = lax.fori_loop(0, chunks, bias_part, jnp.zeros((total, vectors), jnp.float32))
+    for d in range(count):
+        bias_out[d] = acc[d * w_local:(d + 1) * w_local]
+
+    def bias_copy(k):
+        return remote(bias_out.at[peer(k)], bias_in.at[me], bias_send.at[k], bias_recv.at[k], peer(k))
+
+    each(1, count, lambda k: bias_copy(k).start())
+    bias_in[me] = bias_out[me]
+    each(1, count, lambda k: bias_copy(k).wait())
+    summed = jnp.sum(bias_in[...], axis=0)
+    shift = fields[...] - jnp.clip(sqrt_tau * summed, -bias_cap, bias_cap)
+    shift_in[me] = shift.astype(jnp.bfloat16).astype(jnp.float32)
+
+    def shift_copy(k):
+        return remote(shift_in.at[me], shift_in.at[me], shift_send.at[k], shift_recv.at[k], peer(k))
+
+    each(1, count, lambda k: shift_copy(k).start())
+    each(1, count, lambda k: pick_copy(k).wait())
+    flat[...] = jnp.zeros_like(flat)
+    for d in range(count):
+        picks[d * w_local:(d + 1) * w_local, :] = picks_in[d, 0:w_local, :]
+    each(1, count, lambda k: shift_copy(k).wait())
+    for d in range(count):
+        flat[d * w_local:(d + 1) * w_local, :] = shift_in[d]
+    chosen[...] = jnp.dot(
+        picks[...].astype(jnp.bfloat16), flat[...].astype(jnp.bfloat16),
+        preferred_element_type=jnp.float32,
+    ).astype(jnp.bfloat16)
+
+    def pot_copy(c, k):
+        d = peer(k)
+        return remote(
+            pot_out.at[c, pl.ds(d * w_local, w_local)],
+            own.at[:, pl.ds(pl.multiple_of(me * rows + c * tall, tall), tall), :],
+            pot_send.at[c, k], pot_recv.at[c, k], d,
+        )
+
+    for c in range(rows // tall):
+        def one_row(i):
+            columns = pl.ds(pl.multiple_of((c * tall + i) * orbitals, orbitals), orbitals)
+            pot[i] = sqrt_tau * jnp.dot(chosen[...], held[:, columns], preferred_element_type=jnp.float32)
+
+        each(0, tall, one_row)
+        for q in range(0, orbitals, 128):
+            pot_out[c, :, :, q:q + 128] = jnp.swapaxes(pot[:, :, q:q + 128], 0, 1).astype(jnp.bfloat16)
+        each(1, count, lambda k: pot_copy(c, k).start())
+        own[:, pl.ds(pl.multiple_of(me * rows + c * tall, tall), tall), :] = pot_out[c, pl.ds(me * w_local, w_local)]
+
+    halo_copy(0).wait()
+    halo_copy(1).wait()
+    near = (halo.at[0], walkers, halo.at[1])
+    parents = []
+    for j in range(w_local):
+        parent = jnp.zeros((orbitals, occupied), jnp.float32)
+        for s in range(3 * w_local):
+            n = j * 3 * w_local + s
+            parent = parent + weights[n:n + 1, :] * near[s // w_local][s % w_local].astype(jnp.float32)
+        parents.append(parent)
+    for c in range(rows // tall):
+        each(1, count, lambda k: pot_copy(c, k).wait())
+    for j in range(w_local):
+        amat = (own[j].astype(jnp.float32) + one_body[...].astype(jnp.float32)).astype(jnp.bfloat16)
+        term = parents[j].astype(jnp.bfloat16)
+        result = parents[j]
+        for order in range(1, TERMS):
+            product = jnp.dot(amat, term, preferred_element_type=jnp.float32) / order
+            result = result + product
+            term = product.astype(jnp.bfloat16)
+        out[j] = result.astype(jnp.bfloat16)
+
+
+def shards(chol, walkers, trial, one_body, fields, src_shift, src_slot):
+    w_local, orbitals, occupied = walkers.shape
+    vectors, pairs = chol.shape
+    count = lax.axis_size("pair")
+    rows = orbitals // count
+    total = count * w_local
+    if rows % 16 or total > 128 or total % 16 or occupied != 128 or orbitals % 128 or w_local > 4:
+        return plain_shards(chol, walkers, trial, one_body, fields, src_shift, src_slot)
+    chunks = 8
+    tall = 16
+    me = lax.axis_index("pair")
+    source = (me + src_shift + count) % count * w_local + src_slot
+    onehot = (source[:, None] == jnp.arange(128)[None, :]).astype(jnp.float32)
+    onehot = jnp.pad(onehot, ((0, 8 - w_local), (0, 0)))
+    place = (src_shift + 1) * w_local + src_slot
+    weights = (place[:, None] == jnp.arange(3 * w_local)[None, :]).astype(jnp.float32).reshape(-1, 1)
+    weights = jnp.broadcast_to(weights, (weights.shape[0], 128))
+    vmem = pl.BlockSpec(memory_space=pltpu.VMEM)
+    dma = pltpu.SemaphoreType.DMA
+    bf16, f32 = jnp.bfloat16, jnp.float32
+    return pl.pallas_call(
+        functools.partial(step_kernel, count, chunks),
+        out_shape=jax.ShapeDtypeStruct(walkers.shape, bf16),
+        in_specs=[pl.BlockSpec(memory_space=pl.ANY)] + [vmem] * 6,
+        out_specs=vmem,
+        scratch_shapes=[
+            pltpu.VMEM((vectors, pairs), bf16),
+            pltpu.VMEM((count, w_local, rows, occupied), bf16),
+            pltpu.VMEM((2,) + walkers.shape, bf16),
+            pltpu.VMEM((rows, total, orbitals), bf16),
+            pltpu.VMEM((count, 8, 128), f32),
+            pltpu.VMEM((count, w_local, vectors), f32),
+            pltpu.VMEM((count, w_local, vectors), f32),
+            pltpu.VMEM((count, w_local, vectors), f32),
+            pltpu.VMEM((128, vectors), f32),
+            pltpu.VMEM((total, 128), f32),
+            pltpu.VMEM((total, vectors), bf16),
+            pltpu.VMEM((tall, total, orbitals), f32),
+            pltpu.VMEM((rows // tall, total, tall, orbitals), bf16),
+            pltpu.VMEM((w_local, orbitals, orbitals), bf16),
+            dma((chunks,)),
+            dma((count,)), dma((count,)), dma((2,)), dma((2,)), dma((count,)), dma((count,)),
+            dma((count,)), dma((count,)), dma((count,)), dma((count,)),
+            dma((rows // tall, count)), dma((rows // tall, count)),
+        ],
+        compiler_params=pltpu.CompilerParams(
+            collective_id=0, has_side_effects=True, vmem_limit_bytes=52 * 2**20
+        ),
+        cost_estimate=pl.CostEstimate(
+            flops=4 * total * vectors * pairs, bytes_accessed=2 * vectors * pairs, transcendentals=0
+        ),
+    )(chol, walkers, trial, one_body, fields, onehot, weights)
+
+
 def solution(mesh):
     placed = (
         P("groups", "pair"),

time: 120 us -> 75.7 us (0.63)
  Pallas kernels: 0 us -> 69.2 us
  waiting for transfers between devices: 35.8 us -> 0 us
  matrix products: 32.3 us -> 0 us
  starting transfers between devices: 22.7 us -> 0 us
  blocking collectives: 12.3 us -> 0 us
  local copies, waits for them, and re-layouts: 12.6 us -> 4.45 us
    pallas_call x0 -> x1, Pallas kernels: none -> 69.2 us  [shards(): pl.pallas_call(functools.partial(step_kernel, count, chunks), out_shape=j...]
    dot_general x8 -> x0, matrix products: 32.3 us -> none  [the longest x1 15.1 us: shards(): lax.dot_general(green_rows, chol, (((1,), (1,)), ((), ())), preferred_ele...]
    ppermute x2 -> x0, waiting for transfers between devices: 20.9 us -> none  [the longest x1 20.9 us: padded_2(): lax.ppermute(lax.slice_in_dim(block, block.shape[dim] - width, None, axis...]
    all_to_all x4 -> x0, starting transfers between devices: 18.1 us -> none  [the longest x1 7.39 us: shards(): lax.all_to_all(walkers, 'pair', split_axis=1, concat_axis=0, tiled=True)]
    all_to_all x4 -> x0, waiting for transfers between devices: 14.9 us -> none  [the longest x1 8.11 us: shards(): lax.all_to_all(walkers, 'pair', split_axis=1, concat_axis=0, tiled=True)]
    unnamed x1 -> x0, blocking collectives: 12.3 us -> none
    ppermute x2 -> x0, starting transfers between devices: 4.64 us -> none  [the longest x1 4.3 us: padded_2(): lax.ppermute(lax.slice_in_dim(block, 0, width, axis=dim), axis, backward)]
    convert_element_type x2 -> x1, local copies, waits for them, and re-layouts: 4.29 us -> 0.08 us  [shards(): (place[:, None] == jnp.arange(3 * w_local)[None, :]).astype(jnp.float32)]
  transfers between devices with their start and end apart: 6 -> 0, of which waited for: 3 -> 0; matrix products, arithmetic and copies ran while one was open for 2% -> 0% of each run, Pallas kernels for 0% -> 0%
where the time goes in v2:
time: 75.7 us; the launch traced here: 74.5 us
  Pallas kernels  69.2 us (91%)
  local copies, waits for them, and re-layouts  4.45 us (6%)
  other arithmetic  0.84 us (1%)
    pallas_call x1, Pallas kernels, shards(): pl.pallas_call(functools.partial(step_kernel, count, chunks), out_shape=j...  69.2 us
    unnamed x9, local copies, waits for them, and re-layouts  4.3 us

profile of v2, /device:TPU:0, one launch (start us, length us, event | category | flops | bytes accessed | tf_op | source)
XLA Modules:
  0.0 74.5 jit_solution(5677808364520340489)
XLA Ops:
  0.0 0.7 multiply_add_fusion
  0.7 0.1 compare_convert_fusion
  0.8 0.1 reshape.20
  0.8 0.1 iota_compare_fusion
  0.9 0.1 broadcast_in_dim.2.weights
  1.0 0.0 copy-start
  1.0 1.0 %copy-done = bf16[512,512]{1,0:T(8,128)(2,1)S(1)} copy-done((bf16[512,512]{1,0:T(8,128)(2,1)S(1)}, bf16[512,512]{1,0:T(8,128)(2,1)}, u32[]{:S(2)}) %copy-start) | copy-done | bytes 524312
  2.0 0.0 copy-start.1
  2.0 0.9 %copy-done.1 = bf16[2,512,128]{2,1,0:T(8,128)(2,1)S(1)} copy-done((bf16[2,512,128]{2,1,0:T(8,128)(2,1)S(1)}, bf16[2,512,128]{2,1,0:T(8,128)(2,1)}, u32[]{:S(2)}) %copy-start.1) | copy-done | bytes 262168
  3.0 0.0 copy-start.2
  3.0 0.9 %copy-done.2 = bf16[512,128]{1,0:T(8,128)(2,1)S(1)} copy-done((bf16[512,128]{1,0:T(8,128)(2,1)S(1)}, bf16[512,128]{1,0:T(8,128)(2,1)}, u32[]{:S(2)}) %copy-start.2) | copy-done | bytes 131096
  3.9 0.0 copy-start.3
  3.9 0.7 copy-done.3
  4.6 69.2 %shard_map.73 = bf16[2,512,128]{2,1,0:T(8,128)(2,1)S(1)} custom-call(bf16[1024,16384]{1,0:T(8,128)(2,1)} %chol.1, bf16[2,512,128]{2,1,0:T(8,128)(2,1)S(1)} %copy-done.1, bf16[512,128]{1,0:T(8,128)(2,1)S(1)} %copy-done.2, bf16[512,512]{1,0:T(8,128)(2,1)S(1)} %copy-done, f32[2,1024]{1,0:T(2,128)S(1)} %copy-done.3, f32[8,128]{1,0:T(8,128)S(1)} %pad_convert_fusion.onehot, ...), custom_call_target="tpu_custom_call" | custom-call | flops 2147483648 | bytes 33554432 | tf_op jit(solution)/shard_map/pallas_call | solution.py:245
  73.8 0.7 copy.9
  (1 shorter events, 0.0 us)
Async XLA Ops:
  1.0 1.0 %copy-start = (bf16[512,512]{1,0:T(8,128)(2,1)S(1)}, bf16[512,512]{1,0:T(8,128)(2,1)}, u32[]{:S(2)}) copy-start(bf16[512,512]{1,0:T(8,128)(2,1)} %one_body.1) | copy-start | bytes 1572868
  2.0 0.9 %copy-start.1 = (bf16[2,512,128]{2,1,0:T(8,128)(2,1)S(1)}, bf16[2,512,128]{2,1,0:T(8,128)(2,1)}, u32[]{:S(2)}) copy-start(bf16[2,512,128]{2,1,0:T(8,128)(2,1)} %walkers.1) | copy-start | bytes 786436
  3.0 0.9 %copy-start.2 = (bf16[512,128]{1,0:T(8,128)(2,1)S(1)}, bf16[512,128]{1,0:T(8,128)(2,1)}, u32[]{:S(2)}) copy-start(bf16[512,128]{1,0:T(8,128)(2,1)} %trial.1) | copy-start | bytes 393220
  3.9 0.7 copy-start.3

commit v3 on v2

--- a/solution.py
+++ b/solution.py
@@ -74,21 +74,21 @@
 
 
 def step_kernel(
-    count, chunks,
-    chol, walkers, trial, one_body, fields, onehot, weights, out,
-    held, rows_in, halo, green, picks_in, bias_out, bias_in, shift_in, flat, picks,
+    count, chunks, tall,
+    chol, walkers_in, trial_in, body_in, fields, onehot, weights, out,
+    walkers, trial, one_body, held, rows_in, halo, green, picks_in, bias_out, bias_in, shift_in, flat, picks,
     chosen, pot, pot_out, own,
-    load_sem, walk_send, walk_recv, halo_send, halo_recv, pick_send, pick_recv,
-    bias_send, bias_recv, shift_send, shift_recv, pot_send, pot_recv,
+    input_sem, load_sem, walk_send, walk_recv, halo_send, halo_recv, pick_send, pick_recv,
+    bias_send, bias_recv, shift_send, shift_recv, first_send, first_recv, later_send, later_recv,
 ):
     me = lax.axis_index("pair")
     w_local, orbitals, occupied = walkers.shape
     rows = orbitals // count
     total = count * w_local
     vectors, pairs = chol.shape
+    halves = rows // tall
     part = pairs // chunks
     per_part = rows // chunks
-    tall = rows // pot_out.shape[0]
 
     def peer(k):
         return lax.rem(me + k, count)
@@ -106,39 +106,50 @@
     def each(low, high, body):
         lax.fori_loop(low, high, lambda k, carry: (body(k), carry)[1], 0)
 
+    def partners(body):
+        def one(j):
+            body(count // 2 + (2 * lax.rem(j, 2) - 1) * (j // 2))
+
+        each(1, count, one)
+
+    inputs = [
+        pltpu.make_async_copy(source, target, input_sem.at[n])
+        for n, (source, target) in enumerate(
+            ((walkers_in, walkers), (trial_in, trial), (body_in, one_body)))
+    ]
+    inputs[0].start()
+    inputs[1].start()
     each(0, chunks, lambda c: load(c).start())
+    inputs[2].start()
 
     barrier = pltpu.get_barrier_semaphore()
     each(1, count, lambda k: pl.semaphore_signal(
         barrier, inc=1, device_id={"pair": peer(k)}, device_id_type=MESH))
     pl.semaphore_wait(barrier, count - 1)
 
-    def block(d):
-        return pl.ds(pl.multiple_of(d * rows, rows), rows)
-
-    def walk_copy(k):
-        return remote(walkers.at[:, block(peer(k)), :], rows_in.at[me], walk_send.at[k], walk_recv.at[k], peer(k))
+    def block(d, h):
+        return pl.ds(pl.multiple_of(d * rows + h * tall, tall), tall)
+
+    def walk_copy(h, k):
+        return remote(
+            walkers_in.at[:, block(peer(k), h), :], rows_in.at[h, me],
+            walk_send.at[h, k], walk_recv.at[h, k], peer(k),
+        )
 
     def pick_copy(k):
         return remote(onehot, picks_in.at[me], pick_send.at[k], pick_recv.at[k], peer(k))
 
     def halo_copy(side):
         target = peer(1) if side == 0 else peer(count - 1)
-        return remote(walkers, halo.at[side], halo_send.at[side], halo_recv.at[side], target)
-
-    each(1, count, lambda k: walk_copy(k).start())
-    each(1, count, lambda k: pick_copy(k).start())
-    halo_copy(0).start()
-    halo_copy(1).start()
-    rows_in[me] = walkers[:, block(me), :]
+        return remote(walkers_in, halo.at[side], halo_send.at[side], halo_recv.at[side], target)
+
+    for h in range(halves):
+        partners(lambda k: walk_copy(h, k).start())
+    inputs[0].wait()
+    inputs[1].wait()
+    for h in range(halves):
+        rows_in[h, me] = walkers[:, block(me, h), :]
     picks_in[me] = onehot[...]
-    each(1, count, lambda k: walk_copy(k).wait())
-
-    arrived = rows_in[...].astype(jnp.float32).reshape(total, rows, occupied)
-    by_row = jnp.swapaxes(arrived, 0, 1).astype(jnp.bfloat16).reshape(rows * total, occupied)
-    green[...] = lax.dot_general(
-        by_row, trial[...], (((1,), (1,)), ((), ())), preferred_element_type=jnp.float32
-    ).astype(jnp.bfloat16).reshape(rows, total, orbitals)
 
     def bias_part(c, acc):
         load(c).wait()
@@ -150,14 +161,26 @@
             )
         return acc
 
-    acc = lax.fori_loop(0, chunks, bias_part, jnp.zeros((total, vectors), jnp.float32))
+    acc = jnp.zeros((total, vectors), jnp.float32)
+    for h in range(halves):
+        partners(lambda k: walk_copy(h, k).wait())
+        if h == halves - 1:
+            partners(lambda k: pick_copy(k).start())
+            halo_copy(0).start()
+            halo_copy(1).start()
+        arrived = rows_in[h].astype(jnp.float32).reshape(total, tall, occupied)
+        by_row = jnp.swapaxes(arrived, 0, 1).astype(jnp.bfloat16).reshape(tall * total, occupied)
+        green[h * tall:(h + 1) * tall] = lax.dot_general(
+            by_row, trial[...], (((1,), (1,)), ((), ())), preferred_element_type=jnp.float32
+        ).astype(jnp.bfloat16).reshape(tall, total, orbitals)
+        acc = lax.fori_loop(h * chunks // halves, (h + 1) * chunks // halves, bias_part, acc)
     for d in range(count):
         bias_out[d] = acc[d * w_local:(d + 1) * w_local]
 
     def bias_copy(k):
         return remote(bias_out.at[peer(k)], bias_in.at[me], bias_send.at[k], bias_recv.at[k], peer(k))
 
-    each(1, count, lambda k: bias_copy(k).start())
+    partners(lambda k: bias_copy(k).start())
     bias_in[me] = bias_out[me]
     each(1, count, lambda k: bias_copy(k).wait())
     summed = jnp.sum(bias_in[...], axis=0)
@@ -167,7 +190,7 @@
     def shift_copy(k):
         return remote(shift_in.at[me], shift_in.at[me], shift_send.at[k], shift_recv.at[k], peer(k))
 
-    each(1, count, lambda k: shift_copy(k).start())
+    partners(lambda k: shift_copy(k).start())
     each(1, count, lambda k: pick_copy(k).wait())
     flat[...] = jnp.zeros_like(flat)
     for d in range(count):
@@ -180,24 +203,41 @@
         preferred_element_type=jnp.float32,
     ).astype(jnp.bfloat16)
 
-    def pot_copy(c, k):
+    wide = orbitals // 2
+
+    def first_copy(n, k):
+        c, q = n // 2, n % 2 * wide
         d = peer(k)
         return remote(
-            pot_out.at[c, pl.ds(d * w_local, w_local)],
-            own.at[:, pl.ds(pl.multiple_of(me * rows + c * tall, tall), tall), :],
-            pot_send.at[c, k], pot_recv.at[c, k], d,
-        )
-
-    for c in range(rows // tall):
+            pot_out.at[d * w_local, c * tall:(c + 1) * tall, q:q + wide],
+            own.at[0, block(me, c), q:q + wide],
+            first_send.at[n, k], first_recv.at[n, k], d,
+        )
+
+    def later_copy(slot, k):
+        d = peer(k)
+        return remote(
+            pot_out.at[d * w_local + slot],
+            own.at[slot, pl.ds(pl.multiple_of(me * rows, rows), rows), :],
+            later_send.at[slot, k], later_recv.at[slot, k], d,
+        )
+
+    for n in range(2 * halves):
+        c, q = n // 2, n % 2 * wide
+
         def one_row(i):
-            columns = pl.ds(pl.multiple_of((c * tall + i) * orbitals, orbitals), orbitals)
+            columns = pl.ds(pl.multiple_of((c * tall + i) * orbitals + q, wide), wide)
             pot[i] = sqrt_tau * jnp.dot(chosen[...], held[:, columns], preferred_element_type=jnp.float32)
 
         each(0, tall, one_row)
-        for q in range(0, orbitals, 128):
-            pot_out[c, :, :, q:q + 128] = jnp.swapaxes(pot[:, :, q:q + 128], 0, 1).astype(jnp.bfloat16)
-        each(1, count, lambda k: pot_copy(c, k).start())
-        own[:, pl.ds(pl.multiple_of(me * rows + c * tall, tall), tall), :] = pot_out[c, pl.ds(me * w_local, w_local)]
+        for p in range(0, wide, 128):
+            pot_out[:, c * tall:(c + 1) * tall, q + p:q + p + 128] = jnp.swapaxes(
+                pot[:, :, p:p + 128], 0, 1).astype(jnp.bfloat16)
+        partners(lambda k: first_copy(n, k).start())
+    for slot in range(1, w_local):
+        partners(lambda k: later_copy(slot, k).start())
+    for slot in range(w_local):
+        own[slot, pl.ds(pl.multiple_of(me * rows, rows), rows), :] = pot_out[me * w_local + slot]
 
     halo_copy(0).wait()
     halo_copy(1).wait()
@@ -209,9 +249,13 @@
             n = j * 3 * w_local + s
             parent = parent + weights[n:n + 1, :] * near[s // w_local][s % w_local].astype(jnp.float32)
         parents.append(parent)
-    for c in range(rows // tall):
-        each(1, count, lambda k: pot_copy(c, k).wait())
+    inputs[2].wait()
     for j in range(w_local):
+        if j == 0:
+            for n in range(2 * halves):
+                partners(lambda k: first_copy(n, k).wait())
+        else:
+            partners(lambda k: later_copy(j, k).wait())
         amat = (own[j].astype(jnp.float32) + one_body[...].astype(jnp.float32)).astype(jnp.bfloat16)
         term = parents[j].astype(jnp.bfloat16)
         result = parents[j]
@@ -228,7 +272,7 @@
     count = lax.axis_size("pair")
     rows = orbitals // count
     total = count * w_local
-    if rows % 16 or total > 128 or total % 16 or occupied != 128 or orbitals % 128 or w_local > 4:
+    if rows % 16 or 8 % max(rows // 16, 1) or count % 2 or total > 128 or total % 16 or occupied != 128 or orbitals % 256 or w_local > 4:
         return plain_shards(chol, walkers, trial, one_body, fields, src_shift, src_slot)
     chunks = 8
     tall = 16
@@ -243,13 +287,16 @@
     dma = pltpu.SemaphoreType.DMA
     bf16, f32 = jnp.bfloat16, jnp.float32
     return pl.pallas_call(
-        functools.partial(step_kernel, count, chunks),
+        functools.partial(step_kernel, count, chunks, tall),
         out_shape=jax.ShapeDtypeStruct(walkers.shape, bf16),
-        in_specs=[pl.BlockSpec(memory_space=pl.ANY)] + [vmem] * 6,
+        in_specs=[pl.BlockSpec(memory_space=pl.ANY)] * 4 + [vmem] * 3,
         out_specs=vmem,
         scratch_shapes=[
+            pltpu.VMEM(walkers.shape, bf16),
+            pltpu.VMEM(trial.shape, bf16),
+            pltpu.VMEM(one_body.shape, bf16),
             pltpu.VMEM((vectors, pairs), bf16),
-            pltpu.VMEM((count, w_local, rows, occupied), bf16),
+            pltpu.VMEM((rows // tall, count, w_local, tall, occupied), bf16),
             pltpu.VMEM((2,) + walkers.shape, bf16),
             pltpu.VMEM((rows, total, orbitals), bf16),
             pltpu.VMEM((count, 8, 128), f32),
@@ -259,13 +306,14 @@
             pltpu.VMEM((128, vectors), f32),
             pltpu.VMEM((total, 128), f32),
             pltpu.VMEM((total, vectors), bf16),
-            pltpu.VMEM((tall, total, orbitals), f32),
-            pltpu.VMEM((rows // tall, total, tall, orbitals), bf16),
+            pltpu.VMEM((tall, total, orbitals // 2), f32),
+            pltpu.VMEM((total, rows, orbitals), bf16),
             pltpu.VMEM((w_local, orbitals, orbitals), bf16),
-            dma((chunks,)),
-            dma((count,)), dma((count,)), dma((2,)), dma((2,)), dma((count,)), dma((count,)),
+            dma((3,)), dma((chunks,)),
+            dma((rows // tall, count)), dma((rows // tall, count)), dma((2,)), dma((2,)), dma((count,)), dma((count,)),
             dma((count,)), dma((count,)), dma((count,)), dma((count,)),
-            dma((rows // tall, count)), dma((rows // tall, count)),
+            dma((2 * rows // tall, count)), dma((2 * rows // tall, count)),
+            dma((w_local, count)), dma((w_local, count)),
         ],
         compiler_params=pltpu.CompilerParams(
             collective_id=0, has_side_effects=True, vmem_limit_bytes=52 * 2**20

time: 75.7 us -> 73.9 us (0.976); the launches traced: 74.5 us -> 73.7 us
  Pallas kernels: 69.2 us -> 68.4 us
    pallas_call x1, Pallas kernels: 69.2 us -> 68.4 us  [shards(): pl.pallas_call(functools.partial(step_kernel, count, chunks, tall), out_s...]
where the time goes in v3:
time: 73.9 us; the launch traced here: 73.7 us
  Pallas kernels  68.4 us (93%)
  local copies, waits for them, and re-layouts  4.45 us (6%)
  other arithmetic  0.84 us (1%)
    pallas_call x1, Pallas kernels, shards(): pl.pallas_call(functools.partial(step_kernel, count, chunks, tall), out_s...  68.4 us
    unnamed x9, local copies, waits for them, and re-layouts  4.3 us

profile of v3, /device:TPU:0, one launch (start us, length us, event | category | flops | bytes accessed | tf_op | source)
XLA Modules:
  0.0 73.7 jit_solution(6417040748045802415)
XLA Ops:
  0.0 0.7 multiply_add_fusion
  0.7 0.1 compare_convert_fusion
  0.8 0.1 reshape.20
  0.8 0.1 iota_compare_fusion
  0.9 0.1 broadcast_in_dim.2.weights
  1.0 0.0 copy-start
  1.0 1.0 %copy-done = bf16[512,512]{1,0:T(8,128)(2,1)S(1)} copy-done((bf16[512,512]{1,0:T(8,128)(2,1)S(1)}, bf16[512,512]{1,0:T(8,128)(2,1)}, u32[]{:S(2)}) %copy-start) | copy-done | bytes 524312
  2.0 0.0 copy-start.1
  2.0 0.9 %copy-done.1 = bf16[2,512,128]{2,1,0:T(8,128)(2,1)S(1)} copy-done((bf16[2,512,128]{2,1,0:T(8,128)(2,1)S(1)}, bf16[2,512,128]{2,1,0:T(8,128)(2,1)}, u32[]{:S(2)}) %copy-start.1) | copy-done | bytes 262168
  3.0 0.0 copy-start.2
  3.0 0.9 %copy-done.2 = bf16[512,128]{1,0:T(8,128)(2,1)S(1)} copy-done((bf16[512,128]{1,0:T(8,128)(2,1)S(1)}, bf16[512,128]{1,0:T(8,128)(2,1)}, u32[]{:S(2)}) %copy-start.2) | copy-done | bytes 131096
  3.9 0.0 copy-start.3
  3.9 0.7 copy-done.3
  4.6 68.4 %shard_map.73 = bf16[2,512,128]{2,1,0:T(8,128)(2,1)S(1)} custom-call(bf16[1024,16384]{1,0:T(8,128)(2,1)} %chol.1, bf16[2,512,128]{2,1,0:T(8,128)(2,1)S(1)} %copy-done.1, bf16[512,128]{1,0:T(8,128)(2,1)S(1)} %copy-done.2, bf16[512,512]{1,0:T(8,128)(2,1)S(1)} %copy-done, f32[2,1024]{1,0:T(2,128)S(1)} %copy-done.3, f32[8,128]{1,0:T(8,128)S(1)} %pad_convert_fusion.onehot, ...), custom_call_target="tpu_custom_call" | custom-call | flops 2147483648 | bytes 33554432 | tf_op jit(solution)/shard_map/pallas_call | solution.py:289
  73.0 0.7 copy.9
  (1 shorter events, 0.0 us)
Async XLA Ops:
  1.0 1.0 %copy-start = (bf16[512,512]{1,0:T(8,128)(2,1)S(1)}, bf16[512,512]{1,0:T(8,128)(2,1)}, u32[]{:S(2)}) copy-start(bf16[512,512]{1,0:T(8,128)(2,1)} %body_in.1) | copy-start | bytes 1572868
  2.0 0.9 %copy-start.1 = (bf16[2,512,128]{2,1,0:T(8,128)(2,1)S(1)}, bf16[2,512,128]{2,1,0:T(8,128)(2,1)}, u32[]{:S(2)}) copy-start(bf16[2,512,128]{2,1,0:T(8,128)(2,1)} %walkers_in.1) | copy-start | bytes 786436
  3.0 0.9 %copy-start.2 = (bf16[512,128]{1,0:T(8,128)(2,1)S(1)}, bf16[512,128]{1,0:T(8,128)(2,1)}, u32[]{:S(2)}) copy-start(bf16[512,128]{1,0:T(8,128)(2,1)} %trial_in.1) | copy-start | bytes 393220
  3.9 0.7 copy-start.3

commit v4 on v3

--- a/solution.py
+++ b/solution.py
@@ -70,6 +70,8 @@
     return taylor(amat.astype(jnp.bfloat16), parents)
 
 
+SPLITS = 2
+UNROLL = 16
 MESH = pl.DeviceIdType.MESH
 
 
@@ -175,7 +177,8 @@
         ).astype(jnp.bfloat16).reshape(tall, total, orbitals)
         acc = lax.fori_loop(h * chunks // halves, (h + 1) * chunks // halves, bias_part, acc)
     for d in range(count):
-        bias_out[d] = acc[d * w_local:(d + 1) * w_local]
+        for q in range(vectors // 128):
+            bias_out[d, q * w_local:(q + 1) * w_local, :] = acc[d * w_local:(d + 1) * w_local, q * 128:(q + 1) * 128]
 
     def bias_copy(k):
         return remote(bias_out.at[peer(k)], bias_in.at[me], bias_send.at[k], bias_recv.at[k], peer(k))
@@ -185,7 +188,7 @@
     each(1, count, lambda k: bias_copy(k).wait())
     summed = jnp.sum(bias_in[...], axis=0)
     shift = fields[...] - jnp.clip(sqrt_tau * summed, -bias_cap, bias_cap)
-    shift_in[me] = shift.astype(jnp.bfloat16).astype(jnp.float32)
+    shift_in[me] = shift.astype(jnp.bfloat16)
 
     def shift_copy(k):
         return remote(shift_in.at[me], shift_in.at[me], shift_send.at[k], shift_recv.at[k], peer(k))
@@ -197,16 +200,18 @@
         picks[d * w_local:(d + 1) * w_local, :] = picks_in[d, 0:w_local, :]
     each(1, count, lambda k: shift_copy(k).wait())
     for d in range(count):
-        flat[d * w_local:(d + 1) * w_local, :] = shift_in[d]
+        one_shift = shift_in[d].astype(jnp.float32)
+        for q in range(vectors // 128):
+            flat[d * w_local:(d + 1) * w_local, q * 128:(q + 1) * 128] = one_shift[q * w_local:(q + 1) * w_local, :]
     chosen[...] = jnp.dot(
         picks[...].astype(jnp.bfloat16), flat[...].astype(jnp.bfloat16),
         preferred_element_type=jnp.float32,
     ).astype(jnp.bfloat16)
 
-    wide = orbitals // 2
+    wide = orbitals // SPLITS
 
     def first_copy(n, k):
-        c, q = n // 2, n % 2 * wide
+        c, q = n // SPLITS, n % SPLITS * wide
         d = peer(k)
         return remote(
             pot_out.at[d * w_local, c * tall:(c + 1) * tall, q:q + wide],
@@ -222,14 +227,16 @@
             later_send.at[slot, k], later_recv.at[slot, k], d,
         )
 
-    for n in range(2 * halves):
-        c, q = n // 2, n % 2 * wide
-
-        def one_row(i):
-            columns = pl.ds(pl.multiple_of((c * tall + i) * orbitals + q, wide), wide)
-            pot[i] = sqrt_tau * jnp.dot(chosen[...], held[:, columns], preferred_element_type=jnp.float32)
-
-        each(0, tall, one_row)
+    for n in range(SPLITS * halves):
+        c, q = n // SPLITS, n % SPLITS * wide
+
+        def some_rows(g):
+            for u in range(UNROLL):
+                i = g * UNROLL + u
+                columns = pl.ds(pl.multiple_of((c * tall + i) * orbitals + q, wide), wide)
+                pot[i] = sqrt_tau * jnp.dot(chosen[...], held[:, columns], preferred_element_type=jnp.float32)
+
+        each(0, tall // UNROLL, some_rows)
         for p in range(0, wide, 128):
             pot_out[:, c * tall:(c + 1) * tall, q + p:q + p + 128] = jnp.swapaxes(
                 pot[:, :, p:p + 128], 0, 1).astype(jnp.bfloat16)
@@ -252,7 +259,7 @@
     inputs[2].wait()
     for j in range(w_local):
         if j == 0:
-            for n in range(2 * halves):
+            for n in range(SPLITS * halves):
                 partners(lambda k: first_copy(n, k).wait())
         else:
             partners(lambda k: later_copy(j, k).wait())
@@ -272,7 +279,7 @@
     count = lax.axis_size("pair")
     rows = orbitals // count
     total = count * w_local
-    if rows % 16 or 8 % max(rows // 16, 1) or count % 2 or total > 128 or total % 16 or occupied != 128 or orbitals % 256 or w_local > 4:
+    if rows % 16 or vectors % 128 or (w_local * vectors // 128) % 16 or 8 % max(rows // 16, 1) or count % 2 or total > 128 or total % 16 or occupied != 128 or orbitals % 256 or w_local > 4:
         return plain_shards(chol, walkers, trial, one_body, fields, src_shift, src_slot)
     chunks = 8
     tall = 16
@@ -283,6 +290,8 @@
     place = (src_shift + 1) * w_local + src_slot
     weights = (place[:, None] == jnp.arange(3 * w_local)[None, :]).astype(jnp.float32).reshape(-1, 1)
     weights = jnp.broadcast_to(weights, (weights.shape[0], 128))
+    tiles = w_local * vectors // 128
+    laid = fields.reshape(w_local, vectors // 128, 128).swapaxes(0, 1).reshape(tiles, 128)
     vmem = pl.BlockSpec(memory_space=pltpu.VMEM)
     dma = pltpu.SemaphoreType.DMA
     bf16, f32 = jnp.bfloat16, jnp.float32
@@ -300,19 +309,19 @@
             pltpu.VMEM((2,) + walkers.shape, bf16),
             pltpu.VMEM((rows, total, orbitals), bf16),
             pltpu.VMEM((count, 8, 128), f32),
-            pltpu.VMEM((count, w_local, vectors), f32),
-            pltpu.VMEM((count, w_local, vectors), f32),
-            pltpu.VMEM((count, w_local, vectors), f32),
+            pltpu.VMEM((count, tiles, 128), f32),
+            pltpu.VMEM((count, tiles, 128), f32),
+            pltpu.VMEM((count, tiles, 128), bf16),
             pltpu.VMEM((128, vectors), f32),
             pltpu.VMEM((total, 128), f32),
             pltpu.VMEM((total, vectors), bf16),
-            pltpu.VMEM((tall, total, orbitals // 2), f32),
+            pltpu.VMEM((tall, total, orbitals // SPLITS), f32),
             pltpu.VMEM((total, rows, orbitals), bf16),
             pltpu.VMEM((w_local, orbitals, orbitals), bf16),
             dma((3,)), dma((chunks,)),
             dma((rows // tall, count)), dma((rows // tall, count)), dma((2,)), dma((2,)), dma((count,)), dma((count,)),
             dma((count,)), dma((count,)), dma((count,)), dma((count,)),
-            dma((2 * rows // tall, count)), dma((2 * rows // tall, count)),
+            dma((SPLITS * rows // tall, count)), dma((SPLITS * rows // tall, count)),
             dma((w_local, count)), dma((w_local, count)),
         ],
         compiler_params=pltpu.CompilerParams(
@@ -321,7 +330,7 @@
         cost_estimate=pl.CostEstimate(
             flops=4 * total * vectors * pairs, bytes_accessed=2 * vectors * pairs, transcendentals=0
         ),
-    )(chol, walkers, trial, one_body, fields, onehot, weights)
+    )(chol, walkers, trial, one_body, laid, onehot, weights)
 
 
 def solution(mesh):

time: 73.9 us -> 69.4 us (0.939)
  Pallas kernels: 68.4 us -> 63.8 us
    pallas_call x1, Pallas kernels: 68.4 us -> 63.8 us  [shards(): pl.pallas_call(functools.partial(step_kernel, count, chunks, tall), out_s...]
where the time goes in v4:
time: 69.4 us; the launch traced here: 69.1 us
  Pallas kernels  63.8 us (92%)
  local copies, waits for them, and re-layouts  4.45 us (6%)
  other arithmetic  0.84 us (1%)
    pallas_call x1, Pallas kernels, shards(): pl.pallas_call(functools.partial(step_kernel, count, chunks, tall), out_s...  63.8 us
    unnamed x9, local copies, waits for them, and re-layouts  4.3 us

profile of v4, /device:TPU:0, one launch (start us, length us, event | category | flops | bytes accessed | tf_op | source)
XLA Modules:
  0.0 69.1 jit_solution(2381279850965977719)
XLA Ops:
  0.0 0.7 multiply_add_fusion
  0.7 0.1 compare_convert_fusion
  0.8 0.1 reshape.28
  0.8 0.1 iota_compare_fusion
  0.9 0.1 broadcast_in_dim.2.weights
  1.0 0.0 copy-start
  1.0 1.0 %copy-done = bf16[512,512]{1,0:T(8,128)(2,1)S(1)} copy-done((bf16[512,512]{1,0:T(8,128)(2,1)S(1)}, bf16[512,512]{1,0:T(8,128)(2,1)}, u32[]{:S(2)}) %copy-start) | copy-done | bytes 524312
  2.0 0.0 copy-start.1
  2.0 0.9 %copy-done.1 = bf16[2,512,128]{2,1,0:T(8,128)(2,1)S(1)} copy-done((bf16[2,512,128]{2,1,0:T(8,128)(2,1)S(1)}, bf16[2,512,128]{2,1,0:T(8,128)(2,1)}, u32[]{:S(2)}) %copy-start.1) | copy-done | bytes 262168
  3.0 0.0 copy-start.2
  3.0 0.9 %copy-done.2 = bf16[512,128]{1,0:T(8,128)(2,1)S(1)} copy-done((bf16[512,128]{1,0:T(8,128)(2,1)S(1)}, bf16[512,128]{1,0:T(8,128)(2,1)}, u32[]{:S(2)}) %copy-start.2) | copy-done | bytes 131096
  3.9 0.0 copy-start.3
  3.9 0.7 %copy-done.3 = f32[2,1024]{1,0:T(2,128)S(1)} copy-done((f32[2,1024]{1,0:T(2,128)S(1)}, f32[2,1024]{1,0:T(2,128)}, u32[]{:S(2)}) %copy-start.3) | copy-done | bytes 8216
  4.6 63.8 %shard_map.73 = bf16[2,512,128]{2,1,0:T(8,128)(2,1)S(1)} custom-call(bf16[1024,16384]{1,0:T(8,128)(2,1)} %chol.1, bf16[2,512,128]{2,1,0:T(8,128)(2,1)S(1)} %copy-done.1, bf16[512,128]{1,0:T(8,128)(2,1)S(1)} %copy-done.2, bf16[512,512]{1,0:T(8,128)(2,1)S(1)} %copy-done, f32[16,128]{1,0:T(8,128)S(1)} %bitcast.5, f32[8,128]{1,0:T(8,128)S(1)} %pad_convert_fusion.onehot, ...), custom_call_target="tpu_custom_call" | custom-call | flops 2147483648 | bytes 33554432 | tf_op jit(solution)/shard_map/pallas_call | solution.py:298
  68.4 0.7 %copy.10 = bf16[2,512,128]{2,1,0:T(8,128)(2,1)} copy(bf16[2,512,128]{2,1,0:T(8,128)(2,1)S(1)} %shard_map.73) | data formatting | bytes 524288
  (1 shorter events, 0.0 us)
Async XLA Ops:
  1.0 1.0 %copy-start = (bf16[512,512]{1,0:T(8,128)(2,1)S(1)}, bf16[512,512]{1,0:T(8,128)(2,1)}, u32[]{:S(2)}) copy-start(bf16[512,512]{1,0:T(8,128)(2,1)} %body_in.1) | copy-start | bytes 1572868
  2.0 0.9 %copy-start.1 = (bf16[2,512,128]{2,1,0:T(8,128)(2,1)S(1)}, bf16[2,512,128]{2,1,0:T(8,128)(2,1)}, u32[]{:S(2)}) copy-start(bf16[2,512,128]{2,1,0:T(8,128)(2,1)} %walkers_in.1) | copy-start | bytes 786436
  3.0 0.9 %copy-start.2 = (bf16[512,128]{1,0:T(8,128)(2,1)S(1)}, bf16[512,128]{1,0:T(8,128)(2,1)}, u32[]{:S(2)}) copy-start(bf16[512,128]{1,0:T(8,128)(2,1)} %trial_in.1) | copy-start | bytes 393220
  3.9 0.7 %copy-start.3 = (f32[2,1024]{1,0:T(2,128)S(1)}, f32[2,1024]{1,0:T(2,128)}, u32[]{:S(2)}) copy-start(f32[2,1024]{1,0:T(2,128)} %param.11) | copy-start | bytes 24580
